TPU v7x, 32 devices: a whole 2x2x4 slice. The times are simulated.
32 devices in a mesh: groups: 2 (over x), tm: 16 (over z, y, core).
Axes of the slice: x: 2, y: 2, z: 4, core: 2. Of those that a mesh axis runs over, the one named last changes fastest.
Arguments:
- samples: float32 [16384, 2048], P('groups', 'tm'), parts along dimension 0, may hold values from -6 to 6
- test_matrix: float32 [4096, 256], P(('groups', 'tm')), parts along dimension 0, may hold values from -0.125 to 0.125
Outputs:
- basis: float32 [16384, 256], P(('groups', 'tm')), parts along dimension 0
- coordinates: float32 [512, 2048], P('groups', 'tm'), parts along dimension 0
There are 2 independent parts, one for each index of `groups`. A program takes and returns all parts, laid end to end along the dimension named above; each array names one. Nothing has to cross between parts.
All inputs are finite; a program needn't handle non-finite values.
Results may differ from a plain program's by a relative error of at most 0.0003.
Values sent between devices are 32-bit elements; how exact they have to be, the bound alone decides.
A program may use at most 64 MiB of HBM per device.

v0:
```python
import jax
import jax.numpy as jnp
from jax import lax
from jax.sharding import PartitionSpec as P


def local_gram(rows):
    return jnp.dot(
        rows.T, rows, precision=lax.Precision.HIGHEST, preferred_element_type=jnp.float32
    )


def local(samples, test_matrix):
    highest = lax.Precision.HIGHEST
    channels = samples.shape[0]
    sample_rows = samples
    sketch = lax.psum_scatter(
        jnp.dot(sample_rows, test_matrix, precision=highest, preferred_element_type=jnp.float32),
        "tm",
        scatter_dimension=0,
        tiled=True,
    )
    sample_rows = samples
    projected = jnp.einsum(
        "rk,rs->ks",
        lax.all_gather(sketch, "tm", axis=0, tiled=True),
        sample_rows,
        precision=highest,
    )
    gram_one = lax.psum(local_gram(sketch), "tm")
    factor_one = jnp.linalg.cholesky(gram_one)
    orthonormal = jax.scipy.linalg.solve_triangular(factor_one, sketch.T, lower=True).T
    coordinates = jax.scipy.linalg.solve_triangular(factor_one, projected, lower=True)
    return (orthonormal * float(channels) ** 0.5, coordinates)


def solution(mesh):
    placed = (P("groups", "tm"), P(("groups", "tm"), None))
    return jax.shard_map(
        local,
        mesh=mesh,
        in_specs=placed,
        out_specs=(P(("groups", "tm"), None), P("groups", "tm")),
        check_vma=False,
    )
```

profile of v0, /device:TPU:0, one launch (start us, length us, event | category | flops | bytes accessed | tf_op | source)
XLA Modules:
  0.0 320.6 jit_solution(12343590044157621184)
XLA Ops:
  7.2 0.0 copy-start
  7.2 0.0 reduce-scatter.2.cloned.1.call-start
  7.2 0.8 copy-done
  8.1 10.4 %fusion.14 = f32[8192,256]{1,0:T(8,128)} fusion(f32[8192,128]{1,0:T(8,128)} %param.2, f32[128,256]{1,0:T(8,128)S(1)} %copy-done), kind=kOutput, calls=%fused_computation.36 | convolution fusion | flops 3221225472 | bytes 12713984 | tf_op jit(solution)/shard_map/dot_general | solution.py:18
  18.5 0.0 reduce-scatter.2.cloned.1.call-update
  18.5 0.0 all-reduce.3.cloned.1.call-start
  18.5 107.4 %reduce-scatter.2.cloned.1.call-done = f32[512,256]{1,0:T(8,128)} async-done(((f32[8192,256]{1,0:T(8,128)}), f32[512,256]{1,0:T(8,128)}) %reduce-scatter.2.cloned.1.call-update) | async-done | bytes 524304 | tf_op jit(solution)/shard_map/reduce_scatter | solution.py:17
  126.0 0.0 copy-start.1
  126.0 3.0 fusion.15
  128.9 0.0 all-reduce.3.cloned.1.call-update
  128.9 0.2 all-gather.2.cloned.1.call-start
  129.2 0.5 all-gather.2.cloned.1.call-update
  129.7 88.8 %all-reduce.3.cloned.1.call-done = f32[256,256]{0,1:T(8,128)} async-done(((f32[256,256]{0,1:T(8,128)}), f32[256,256]{0,1:T(8,128)}) %all-reduce.3.cloned.1.call-update) | async-done | bytes 262160 | tf_op jit(solution)/shard_map/psum | solution.py:30
  218.5 1.1 copy.5
  219.6 1.0 fusion.3
  220.6 11.7 %cholesky.50 = f32[128,128]{1,0:T(8,128)S(1)} custom-call(f32[128,128]{1,0:T(8,128)S(1)} %cholesky.118), custom_call_target="Cholesky" | custom-call | tf_op jit(solution)/shard_map/jit(cholesky)/cholesky | solution.py:31
  232.3 9.8 %custom-call.18 = f32[1,128,128]{1,2,0:T(8,128)S(1)} custom-call(f32[1,128,128]{2,1,0:T(8,128)S(1)} %get-tuple-element.25), custom_call_target="InvertDiagBlocksLowerTriangular" | custom-call | tf_op jit(solution)/shard_map/jit(cholesky)/cholesky | solution.py:31
  242.1 0.2 constant_dynamic-update-slice_fusion.1
  242.4 0.3 convolution_subtract_fusion.2
  242.6 11.7 %cholesky.105 = f32[128,128]{1,0:T(8,128)S(1)} custom-call(f32[128,128]{1,0:T(8,128)S(1)} %convolution_subtract_fusion.2), custom_call_target="Cholesky" | custom-call | tf_op jit(solution)/shard_map/jit(cholesky)/cholesky | solution.py:31
  254.4 0.7 compare_reduce_fusion
  256.4 0.1 triangular_solve.72
  256.5 4.1 %while.1 = (s32[]{:T(128)}, f32[256,256]{1,0:T(8,128)S(1)}, s32[2,2]{1,0:T(2,128)S(1)}, f32[2,128,128]{2,1,0:T(8,128)S(1)}, s32[]{:T(128)}) while((s32[]{:T(128)}, f32[256,256]{1,0:T(8,128)S(1)}, s32[2,2]{1,0:T(2,128)S(1)}, f32[2,128,128]{2,1,0:T(8,128)S(1)}, s32[]{:T(128)}) %tuple.28), condition=%wide.while_cond, body=%wide.while_body.sunk | while | flops 2 | bytes 131189 | solution.py:32
  256.6 0.6 fusion.30
  257.2 1.4 bitcast_dynamic-update-slice_fusion.2
  258.6 0.6 fusion.30
  259.2 1.4 bitcast_dynamic-update-slice_fusion.2
  260.6 19.7 %custom-call.19 = f32[2,128,128]{1,2,0:T(8,128)S(1)} custom-call(f32[2,128,128]{2,1,0:T(8,128)S(1)} %get-tuple-element.9), custom_call_target="InvertDiagBlocksLowerTriangular" | custom-call | tf_op jit(solution)/shard_map/jit(_solve_triangular)/triangular_solve | solution.py:32
  280.3 0.0 copy-done.1
  280.3 0.4 fusion.1
  280.7 0.6 convolution_subtract_fusion
  281.3 0.4 fusion.10
  281.8 0.1 fusion
  281.8 1.0 copy.6
  282.8 13.6 %all-gather.2.cloned.1.call-done = f32[8192,256]{1,0:T(8,128)} async-done(((f32[512,256]{1,0:T(8,128)}), f32[8192,256]{1,0:T(8,128)}) %all-gather.2.cloned.1.call-update) | async-done | bytes 8388624 | tf_op jit(solution)/shard_map/all_gather | solution.py:26
  296.4 16.2 %fusion.16 = f32[256,128]{1,0:T(8,128)S(1)} fusion(f32[8192,256]{1,0:T(8,128)} %all-gather.2.cloned.1.call-done, f32[8192,128]{1,0:T(8,128)} %param.2), kind=kOutput, calls=%fused_computation.38 | convolution fusion | flops 3221225472 | bytes 12713984 | tf_op jit(solution)/shard_map/rk,rs->ks/dot_general | solution.py:24
  312.6 0.3 fusion.4
  312.9 0.2 convolution_subtract_fusion.1
  313.1 0.3 fusion.9
  313.4 0.7 pad_maximum_fusion
  (9 shorter events, 0.1 us)
Async XLA Ops:
  7.2 0.9 copy-start
  7.2 118.8 %reduce-scatter.2.cloned.1.call-start = ((), (), s32[]{:S(2)}) async-start(), calls=%async_computation.1 | async-start | bytes 8912896 | tf_op jit(solution)/shard_map/reduce_scatter | solution.py:17
  18.5 200.0 %all-reduce.3.cloned.1.call-start = ((), (), s32[]{:S(2)}) async-start(), calls=%async_computation.2 | async-start | bytes 524288 | tf_op jit(solution)/shard_map/psum | solution.py:30
  126.0 154.3 %copy-start.1 = (f32[512,256]{1,0:T(8,128)S(1)}, f32[512,256]{1,0:T(8,128)}, u32[]{:S(2)}) copy-start(f32[512,256]{1,0:T(8,128)} %reduce-scatter.2.cloned.1.call-done) | copy-start | bytes 1572868
  128.9 167.4 %all-gather.2.cloned.1.call-start = ((), (), s32[]{:S(2)}) async-start(), calls=%async_computation.3 | async-start | bytes 8912896 | tf_op jit(solution)/shard_map/all_gather | solution.py:26
Sparse Core Ops, SparseCore 0:
  18.6 107.2 reduce-scatter.1
  129.9 88.5 all-reduce.2
  220.6 75.6 all-gather.1
where the time goes:
time: 321 us
  waiting for transfers between devices  210 us (65%)
  other arithmetic  55.4 us (17%)
  matrix products  32.2 us (10%)
  between operations  15.2 us (5%)
  local copies, waits for them, and re-layouts  6.96 us (2%)
    reduce_scatter x1, waiting for transfers between devices, local(): lax.psum_scatter(jnp.dot(sample_rows, test_matrix, precision=highest, pre...  107 us
    psum x1, waiting for transfers between devices, local(): gram_one = lax.psum(local_gram(sketch), 'tm')  88.8 us
    another operation x6, other arithmetic, local(): factor_one = jnp.linalg.cholesky(gram_one)  34 us
    another operation x3, other arithmetic, local(): jax.scipy.linalg.solve_triangular(factor_one, sketch.T, lower=True)  19.7 us
    dot_general x1, matrix products, local(): jnp.einsum('rk,rs->ks', lax.all_gather(sketch, 'tm', axis=0, tiled=True),...  16.2 us
    all_gather x1, waiting for transfers between devices, local(): lax.all_gather(sketch, 'tm', axis=0, tiled=True)  13.6 us
    dot_general x1, matrix products, local(): jnp.dot(sample_rows, test_matrix, precision=highest, preferred_element_ty...  10.4 us
  transfers between devices with their start and end apart: 3, of which 3 were waited for; matrix products, arithmetic and copies ran while one was open for 20% of the time, Pallas kernels for 0%

commit v1 on v0

v1 whole, which is shorter than its diff:
```python
import functools

import jax
import jax.numpy as jnp
from jax import lax
from jax.experimental import pallas as pl
from jax.experimental.pallas import tpu as pltpu
from jax.sharding import PartitionSpec as P

HIGHEST = lax.Precision.HIGHEST
PLANE = 4
AHEAD = 4


def exchange_kernel(
    line, parts, sub, a_ref, o_ref, y_out, g_out, p_out,
    abuf, obuf, part, arrived, full, acc, from_core, from_y,
    a_send, a_recv, o_send, o_recv, rs_send, rs_recv, ag_send, ag_recv, fin_send, fin_recv,
):
    width = a_ref.shape[1]
    rank = o_ref.shape[1]
    rows = parts * sub
    me = lax.axis_index("tm")
    z = me // PLANE
    p = me % PLANE
    y, core = p // 2, p % 2
    base = z * PLANE
    place = (p, (1 - y) * 2 + core, y * 2 + 1 - core, (1 - y) * 2 + 1 - core)

    def remote(src, dst, send, recv, target):
        return pltpu.make_async_remote_copy(
            src_ref=src, dst_ref=dst, send_sem=send, recv_sem=recv,
            device_id={"tm": target}, device_id_type=pl.DeviceIdType.MESH,
        )

    def a_copy(d, w, j):
        start = pl.multiple_of((w * PLANE + place[d]) * rows + j * sub, sub)
        return remote(
            a_ref.at[pl.ds(start, sub), :],
            abuf.at[w, pl.ds(pl.multiple_of(j * sub, sub), sub), pl.ds(d * width, width)],
            a_send.at[d - 1, w, j], a_recv.at[d - 1, w, j], base + place[d],
        )

    def o_copy(d):
        return remote(
            o_ref, obuf.at[pl.ds(d * width, width), :], o_send.at[d - 1], o_recv.at[d - 1], base + place[d]
        )

    def at(ref, w, j):
        return ref.at[w, pl.ds(pl.multiple_of(j * sub, sub), sub), :]

    def rs_copy(way, w, j):
        return remote(
            at(part, w, j), arrived.at[way, w, pl.ds(pl.multiple_of(j * sub, sub), sub), :],
            rs_send.at[w, j], rs_recv.at[way, w, j], me + (PLANE if way == 0 else -PLANE),
        )

    def ag_copy(way, w, j):
        return remote(
            at(full, w, j), at(full, w, j),
            ag_send.at[way, w, j], ag_recv.at[w, j], me + (PLANE if way == 0 else -PLANE),
        )

    has_left, has_right = z > 0, z < line - 1
    barrier = pltpu.get_barrier_semaphore()

    def greet(target):
        pl.semaphore_signal(barrier, inc=1, device_id={"tm": target}, device_id_type=pl.DeviceIdType.MESH)

    for d in range(1, PLANE):
        greet(base + place[d])

    @pl.when(has_left)
    def _():
        greet(me - PLANE)

    @pl.when(has_right)
    def _():
        greet(me + PLANE)

    pl.semaphore_wait(barrier, PLANE - 1 + has_left.astype(jnp.int32) + has_right.astype(jnp.int32))

    for d in (1, 3, 2):
        o_copy(d).start()

    def send_a(step):
        t, j = step // parts, step % parts

        def go(w):
            for d in (1, 3, 2):
                a_copy(d, w, j).start()

        @pl.when(line - 1 - t > z)
        def _():
            go(line - 1 - t)

        @pl.when(jnp.logical_and(t < z, t < line - 1))
        def _():
            go(t)

        @pl.when(t == line - 1)
        def _():
            go(z)

    steps = line * parts
    ahead = min(AHEAD, steps)
    for s in range(ahead):
        send_a(jnp.int32(s))

    def keep_own(w, _):
        start = pl.multiple_of((w * PLANE + p) * rows, rows)
        abuf[w, :, pl.ds(0, width)] = a_ref[pl.ds(start, rows), :]
        return 0

    lax.fori_loop(0, line, keep_own, 0)
    obuf[pl.ds(0, width), :] = o_ref[...]
    acc[...] = jnp.zeros_like(acc)
    for d in range(1, PLANE):
        o_copy(d).wait_recv()

    def product(w, j):
        for d in range(1, PLANE):
            a_copy(d, w, j).wait_recv()
        return jnp.dot(at(abuf, w, j)[...], obuf[...], precision=HIGHEST, preferred_element_type=jnp.float32)

    def use(w, j):
        block = at(full, w, j)[...]
        both = jnp.concatenate([block, at(abuf, w, j)[...]], axis=1)
        acc[...] += lax.dot_general(
            block, both, (((0,), (0,)), ((), ())), precision=HIGHEST, preferred_element_type=jnp.float32
        )

    def reduce_step(step, _):
        @pl.when(step + ahead < steps)
        def _():
            send_a(step + ahead)

        t, j = step // parts, step % parts

        def pass_on(way, w, inner):
            at(part, w, j)[...] = product(w, j)

            @pl.when(inner)
            def _():
                rs_copy(way, w, j).wait_recv()
                at(part, w, j)[...] += arrived[way, w, pl.ds(pl.multiple_of(j * sub, sub), sub), :]

            rs_copy(way, w, j).start()

        @pl.when(line - 1 - t > z)
        def _():
            pass_on(0, line - 1 - t, has_left)

        @pl.when(jnp.logical_and(t < z, t < line - 1))
        def _():
            pass_on(1, t, has_right)

        @pl.when(t == line - 1)
        def _():
            at(full, z, j)[...] = product(z, j)

            @pl.when(has_left)
            def _():
                rs_copy(0, z, j).wait_recv()
                at(full, z, j)[...] += arrived[0, z, pl.ds(pl.multiple_of(j * sub, sub), sub), :]

            @pl.when(has_right)
            def _():
                rs_copy(1, z, j).wait_recv()
                at(full, z, j)[...] += arrived[1, z, pl.ds(pl.multiple_of(j * sub, sub), sub), :]
                ag_copy(0, z, j).start()

            @pl.when(has_left)
            def _():
                ag_copy(1, z, j).start()

            use(z, j)

        return 0

    lax.fori_loop(0, steps, reduce_step, 0)
    y_out[...] = full[z]

    def gather_step(step, _):
        t, j = step // parts + 1, step % parts

        @pl.when(t <= z)
        def _():
            w = z - t
            ag_copy(0, w, j).wait_recv()

            @pl.when(has_right)
            def _():
                ag_copy(0, w, j).start()

            use(w, j)

        @pl.when(z + t < line)
        def _():
            w = z + t
            ag_copy(1, w, j).wait_recv()

            @pl.when(has_left)
            def _():
                ag_copy(1, w, j).start()

            use(w, j)

        return 0

    lax.fori_loop(0, (line - 1) * parts, gather_step, 0)

    two = 2 * width
    core_copies = (
        remote(acc.at[:, pl.ds(0, rank)], from_core.at[:, pl.ds(0, rank)],
               fin_send.at[0], fin_recv.at[0], base + place[2]),
        remote(acc.at[:, pl.ds(rank + two, two)], from_core.at[:, pl.ds(rank, two)],
               fin_send.at[1], fin_recv.at[1], base + place[2]),
    )
    for copy in core_copies:
        copy.start()
    for copy in core_copies:
        copy.wait()
    acc[:, pl.ds(0, rank + two)] += from_core[...]
    y_copies = (
        remote(acc.at[:, pl.ds(0, rank)], from_y.at[:, pl.ds(0, rank)],
               fin_send.at[2], fin_recv.at[2], base + place[1]),
        remote(acc.at[:, pl.ds(rank + width, width)], from_y.at[:, pl.ds(rank, width)],
               fin_send.at[3], fin_recv.at[3], base + place[1]),
    )
    for copy in y_copies:
        copy.start()
    for copy in y_copies:
        copy.wait()
    g_out[...] = acc[:, pl.ds(0, rank)] + from_y[:, pl.ds(0, rank)]
    p_out[...] = acc[:, pl.ds(rank, width)] + from_y[:, pl.ds(rank, width)]

    for d in range(1, PLANE):
        o_copy(d).wait_send()

    def drain(step, _):
        w, j = step // parts, step % parts
        for d in range(1, PLANE):
            a_copy(d, w, j).wait_send()

        @pl.when(w != z)
        def _():
            rs_copy(0, w, j).wait_send()

        @pl.when(jnp.logical_and(has_right, w <= z))
        def _():
            ag_copy(0, w, j).wait_send()

        @pl.when(jnp.logical_and(has_left, w >= z))
        def _():
            ag_copy(1, w, j).wait_send()

        return 0

    lax.fori_loop(0, steps, drain, 0)


def exchange(n, samples, test_matrix):
    channels, width = samples.shape
    rank = test_matrix.shape[1]
    line = n // PLANE
    rows = channels // n
    sub = min(128, rows)
    parts = rows // sub
    f32 = jnp.float32
    dma = pltpu.SemaphoreType.DMA
    vmem = pl.BlockSpec(memory_space=pltpu.VMEM)
    return pl.pallas_call(
        functools.partial(exchange_kernel, line, parts, sub),
        out_shape=(
            jax.ShapeDtypeStruct((rows, rank), f32),
            jax.ShapeDtypeStruct((rank, rank), f32),
            jax.ShapeDtypeStruct((rank, width), f32),
        ),
        in_specs=[vmem] * 2,
        out_specs=(vmem,) * 3,
        scratch_shapes=[
            pltpu.VMEM((line, rows, PLANE * width), f32),
            pltpu.VMEM((PLANE * width, rank), f32),
            pltpu.VMEM((line, rows, rank), f32),
            pltpu.VMEM((2, line, rows, rank), f32),
            pltpu.VMEM((line, rows, rank), f32),
            pltpu.VMEM((rank, rank + PLANE * width), f32),
            pltpu.VMEM((rank, rank + 2 * width), f32),
            pltpu.VMEM((rank, rank + width), f32),
            dma((PLANE - 1, line, parts)),
            dma((PLANE - 1, line, parts)),
            dma((PLANE - 1,)),
            dma((PLANE - 1,)),
            dma((line, parts)),
            dma((2, line, parts)),
            dma((2, line, parts)),
            dma((line, parts)),
            dma((4,)),
            dma((4,)),
        ],
        compiler_params=pltpu.CompilerParams(
            collective_id=0, has_side_effects=True, vmem_limit_bytes=40 * 1024 * 1024
        ),
    )(samples, test_matrix)


def local(n, samples, test_matrix):
    channels = samples.shape[0]
    sketch, gram, projected = exchange(n, samples, test_matrix)
    factor = jnp.linalg.cholesky(gram)
    orthonormal = jax.scipy.linalg.solve_triangular(factor, sketch.T, lower=True).T
    coordinates = jax.scipy.linalg.solve_triangular(factor, projected, lower=True)
    return (orthonormal * float(channels) ** 0.5, coordinates)


def solution(mesh):
    placed = (P("groups", "tm"), P(("groups", "tm"), None))
    return jax.shard_map(
        functools.partial(local, mesh.shape["tm"]),
        mesh=mesh,
        in_specs=placed,
        out_specs=(P(("groups", "tm"), None), P("groups", "tm")),
        check_vma=False,
    )
```

time: 321 us -> 184 us (0.57)
  waiting for transfers between devices: 210 us -> 0 us
  Pallas kernels: 0 us -> 116 us
  matrix products: 32.2 us -> 2.66 us
  between operations: 15.2 us -> 2.09 us
    pallas_call x0 -> x1, Pallas kernels: none -> 116 us  [exchange(): pl.pallas_call(functools.partial(exchange_kernel, line, parts, sub), out_...]
    reduce_scatter x1 -> x0, waiting for transfers between devices: 107 us -> none  [local(): lax.psum_scatter(jnp.dot(sample_rows, test_matrix, precision=highest, pre...]
    psum x1 -> x0, waiting for transfers between devices: 88.8 us -> none  [local(): gram_one = lax.psum(local_gram(sketch), 'tm')]
    dot_general x3 -> x0, matrix products: 29.6 us -> none  [the longest x1 16.2 us: local(): jnp.einsum('rk,rs->ks', lax.all_gather(sketch, 'tm', axis=0, tiled=True),...]
    all_gather x1 -> x0, waiting for transfers between devices: 13.6 us -> none  [local(): lax.all_gather(sketch, 'tm', axis=0, tiled=True)]
  transfers between devices with their start and end apart: 3 -> 0, of which waited for: 3 -> 0; matrix products, arithmetic and copies ran while one was open for 20% -> 0% of each run, Pallas kernels for 0% -> 0%
where the time goes in v1:
time: 184 us
  Pallas kernels  116 us (63%)
  other arithmetic  54.6 us (30%)
  local copies, waits for them, and re-layouts  8.37 us (5%)
  matrix products  2.66 us (1%)
  between operations  2.09 us (1%)
    pallas_call x1, Pallas kernels, exchange(): pl.pallas_call(functools.partial(exchange_kernel, line, parts, sub), out_...  116 us
    another operation x6, other arithmetic, local(): factor = jnp.linalg.cholesky(gram)  34 us
    another operation x3, other arithmetic, local(): jax.scipy.linalg.solve_triangular(factor, sketch.T, lower=True)  19.9 us
    unnamed x5, local copies, waits for them, and re-layouts  4.08 us
    another operation x6, local copies, waits for them, and re-layouts  4.06 us

profile of v1, /device:TPU:0, one launch (start us, length us, event | category | flops | bytes accessed | tf_op | source)
XLA Modules:
  0.0 183.7 jit_solution(18369959254346005202)
XLA Ops:
  0.6 0.0 copy-start
  0.6 2.2 %copy-done = f32[8192,128]{1,0:T(8,128)S(1)} copy-done((f32[8192,128]{1,0:T(8,128)S(1)}, f32[8192,128]{1,0:T(8,128)}, u32[]{:S(2)}) %copy-start) | copy-done | bytes 4194328
  2.8 0.0 copy-start.1
  2.8 0.9 copy-done.1
  3.7 115.9 %shard_map.41 = (f32[512,256]{1,0:T(8,128)S(1)}, f32[256,256]{1,0:T(8,128)S(1)}, f32[256,128]{1,0:T(8,128)S(1)}) custom-call(f32[8192,128]{1,0:T(8,128)S(1)} %copy-done, f32[128,256]{1,0:T(8,128)S(1)} %copy-done.1), custom_call_target="tpu_custom_call" | custom-call | tf_op jit(solution)/shard_map/pallas_call | solution.py:273
  119.6 0.1 copy.4
  119.8 11.7 %cholesky.50 = f32[128,128]{1,0:T(8,128)S(1)} custom-call(f32[128,128]{1,0:T(8,128)S(1)} %cholesky.118), custom_call_target="Cholesky" | custom-call | tf_op jit(solution)/shard_map/jit(cholesky)/cholesky | solution.py:311
  131.6 9.8 %custom-call.18 = f32[1,128,128]{1,2,0:T(8,128)S(1)} custom-call(f32[1,128,128]{2,1,0:T(8,128)S(1)} %get-tuple-element.31), custom_call_target="InvertDiagBlocksLowerTriangular" | custom-call | tf_op jit(solution)/shard_map/jit(cholesky)/cholesky | solution.py:311
  141.4 0.2 constant_dynamic-update-slice_fusion.1
  141.6 0.3 convolution_subtract_fusion.2
  141.9 11.7 %cholesky.105 = f32[128,128]{1,0:T(8,128)S(1)} custom-call(f32[128,128]{1,0:T(8,128)S(1)} %convolution_subtract_fusion.2), custom_call_target="Cholesky" | custom-call | tf_op jit(solution)/shard_map/jit(cholesky)/cholesky | solution.py:311
  153.7 0.6 compare_reduce_fusion
  155.7 0.1 triangular_solve.72
  155.7 4.1 %while.1 = (s32[]{:T(128)}, f32[256,256]{1,0:T(8,128)S(1)}, s32[2,2]{1,0:T(2,128)S(1)}, f32[2,128,128]{2,1,0:T(8,128)S(1)}, s32[]{:T(128)}) while((s32[]{:T(128)}, f32[256,256]{1,0:T(8,128)S(1)}, s32[2,2]{1,0:T(2,128)S(1)}, f32[2,128,128]{2,1,0:T(8,128)S(1)}, s32[]{:T(128)}) %tuple.28), condition=%wide.while_cond, body=%wide.while_body.sunk | while | flops 2 | bytes 131181 | solution.py:312
  155.7 0.6 fusion.21
  156.3 1.4 bitcast_dynamic-update-slice_fusion.2
  157.8 0.6 fusion.21
  158.4 1.4 bitcast_dynamic-update-slice_fusion.2
  159.8 19.9 %custom-call.19 = f32[2,128,128]{1,2,0:T(8,128)S(1)} custom-call(f32[2,128,128]{2,1,0:T(8,128)S(1)} %get-tuple-element.15), custom_call_target="InvertDiagBlocksLowerTriangular" | custom-call | tf_op jit(solution)/shard_map/jit(_solve_triangular)/triangular_solve | solution.py:312
  179.7 0.3 fusion.7
  180.0 0.2 convolution_subtract_fusion.1
  180.2 0.3 fusion.9
  180.5 0.7 pad_maximum_fusion
  181.2 0.4 fusion.1
  181.6 0.6 convolution_subtract_fusion
  182.2 0.4 fusion.10
  182.6 0.1 fusion
  182.7 1.0 copy.5
  (10 shorter events, 0.2 us)
Async XLA Ops:
  0.6 2.2 %copy-start = (f32[8192,128]{1,0:T(8,128)S(1)}, f32[8192,128]{1,0:T(8,128)}, u32[]{:S(2)}) copy-start(f32[8192,128]{1,0:T(8,128)} %a_ref.1) | copy-start | bytes 12582916
  2.8 0.9 copy-start.1

commit v2 on v1

--- a/solution.py
+++ b/solution.py
@@ -305,13 +305,81 @@
     )(samples, test_matrix)
 
 
+def dot(a, b, contract=(1, 0)):
+    return lax.dot_general(
+        a, b, (((contract[0],), (contract[1],)), ((), ())), precision=HIGHEST, preferred_element_type=jnp.float32
+    )
+
+
+def inverse_factor(gram):
+    n = gram.shape[0]
+    blocks = n // 8
+    row = lax.broadcasted_iota(jnp.int32, (8, n), 0)
+    lane = lax.broadcasted_iota(jnp.int32, (8, n), 1)
+    left = [gram[8 * i : 8 * i + 8, :] for i in range(blocks)]
+    right = [jnp.where(lane == row + 8 * i, 1.0, 0.0) for i in range(blocks)]
+
+    def spread(block, j):
+        return jnp.broadcast_to(block[j : j + 1, :], (8, n))
+
+    done = []
+    for g in range(blocks):
+        cols = {
+            i: [jnp.broadcast_to(left[i][:, 8 * g + j : 8 * g + j + 1], (8, n)) for j in range(8)]
+            for i in range(g, blocks)
+        }
+        scale = jnp.zeros((8, n), jnp.float32)
+        for j in range(8):
+            pivot = spread(cols[g][j], j)
+            inverse = 1.0 / pivot
+            scale = jnp.where(row == j, lax.rsqrt(pivot), scale)
+            across = [spread(cols[g][j], l) for l in range(8)]
+            left_row, right_row = spread(left[g], j), spread(right[g], j)
+            for i in range(g, blocks):
+                times = cols[i][j] * inverse
+                if i == g:
+                    times = jnp.where(row > j, times, 0.0)
+                for l in range(j + 1, 8):
+                    cols[i][l] = cols[i][l] - times * across[l]
+                left[i] = left[i] - times * left_row
+                right[i] = right[i] - times * right_row
+        done.append(right[g] * scale)
+    return jnp.concatenate(done, axis=0)
+
+
+def inverse_of(gram):
+    rank = gram.shape[0]
+    if rank <= 128:
+        return inverse_factor(gram)
+    half = rank // 2
+    first = inverse_of(gram[:half, :half])
+    lower = dot(gram[half:, :half], first, (1, 1))
+    second = inverse_of(gram[half:, half:] - dot(lower, lower, (1, 1)))
+    corner = -dot(second, dot(lower, first))
+    top = jnp.concatenate([first, jnp.zeros_like(first)], axis=1)
+    return jnp.concatenate([top, jnp.concatenate([corner, second], axis=1)], axis=0)
+
+
+def factor_kernel(root, y_ref, g_ref, p_ref, basis_ref, coordinates_ref):
+    inverse = inverse_of(g_ref[...])
+    basis_ref[...] = dot(y_ref[...], inverse, (1, 1)) * root
+    coordinates_ref[...] = dot(inverse, p_ref[...])
+
+
 def local(n, samples, test_matrix):
     channels = samples.shape[0]
     sketch, gram, projected = exchange(n, samples, test_matrix)
-    factor = jnp.linalg.cholesky(gram)
-    orthonormal = jax.scipy.linalg.solve_triangular(factor, sketch.T, lower=True).T
-    coordinates = jax.scipy.linalg.solve_triangular(factor, projected, lower=True)
-    return (orthonormal * float(channels) ** 0.5, coordinates)
+    vmem = pl.BlockSpec(memory_space=pltpu.VMEM)
+    return pl.pallas_call(
+        functools.partial(factor_kernel, float(channels) ** 0.5),
+        out_shape=(
+            jax.ShapeDtypeStruct(sketch.shape, jnp.float32),
+            jax.ShapeDtypeStruct(projected.shape, jnp.float32),
+        ),
+        in_specs=[vmem] * 3,
+        out_specs=(vmem,) * 2,
+        compiler_params=pltpu.CompilerParams(vmem_limit_bytes=16 * 1024 * 1024),
+    )(sketch, gram, projected)
 
 
 def solution(mesh):

time: 184 us -> 131 us (0.71)
  other arithmetic: 54.6 us -> 0 us
  Pallas kernels: 116 us -> 127 us
  local copies, waits for them, and re-layouts: 8.37 us -> 3.08 us
  matrix products: 2.66 us -> 0 us
    another operation x10 -> x0, other arithmetic: 54.5 us -> none  [the longest x6 34 us: local(): factor = jnp.linalg.cholesky(gram)]
    pallas_call x0 -> x1, Pallas kernels: none -> 10.9 us  [local(): pl.pallas_call(functools.partial(factor_kernel, float(channels) ** 0.5),...]
    another operation x9 -> x0, local copies, waits for them, and re-layouts: 4.16 us -> none
    another operation x8 -> x0, matrix products: 2.66 us -> none  [the longest x3 1.42 us: local(): jax.scipy.linalg.solve_triangular(factor, sketch.T, lower=True)]
    unnamed x5 -> x4, local copies, waits for them, and re-layouts: 4.08 us -> 3.08 us
where the time goes in v2:
time: 131 us; the launch traced here: 130 us
  Pallas kernels  127 us (97%)
  local copies, waits for them, and re-layouts  3.08 us (2%)
    pallas_call x1, Pallas kernels, exchange(): pl.pallas_call(functools.partial(exchange_kernel, line, parts, sub), out_...  116 us
    pallas_call x1, Pallas kernels, local(): pl.pallas_call(functools.partial(factor_kernel, float(channels) ** 0.5),...  10.9 us
    unnamed x4, local copies, waits for them, and re-layouts  3.08 us

profile of v2, /device:TPU:0, one launch (start us, length us, event | category | flops | bytes accessed | tf_op | source)
XLA Modules:
  0.0 130.5 jit_solution(13043180985735053607)
XLA Ops:
  0.6 0.0 copy-start
  0.6 2.2 %copy-done = f32[8192,128]{1,0:T(8,128)S(1)} copy-done((f32[8192,128]{1,0:T(8,128)S(1)}, f32[8192,128]{1,0:T(8,128)}, u32[]{:S(2)}) %copy-start) | copy-done | bytes 4194328
  2.8 0.0 copy-start.1
  2.8 0.9 copy-done.1
  3.7 115.8 %shard_map.41 = (f32[512,256]{1,0:T(8,128)S(1)}, f32[256,256]{1,0:T(8,128)S(1)}, f32[256,128]{1,0:T(8,128)S(1)}) custom-call(f32[8192,128]{1,0:T(8,128)S(1)} %copy-done, f32[128,256]{1,0:T(8,128)S(1)} %copy-done.1), custom_call_target="tpu_custom_call" | custom-call | tf_op jit(solution)/shard_map/pallas_call | solution.py:273
  119.6 10.9 %shard_map.42 = (f32[512,256]{1,0:T(8,128)}, f32[256,128]{1,0:T(8,128)}) custom-call(f32[512,256]{1,0:T(8,128)S(1)} %get-tuple-element.5.y_ref, f32[256,256]{1,0:T(8,128)S(1)} %get-tuple-element.6.g_ref, f32[256,128]{1,0:T(8,128)S(1)} %get-tuple-element.7.p_ref), custom_call_target="tpu_custom_call" | custom-call | tf_op jit(solution)/shard_map/pallas_call | solution.py:373
Async XLA Ops:
  0.6 2.2 %copy-start = (f32[8192,128]{1,0:T(8,128)S(1)}, f32[8192,128]{1,0:T(8,128)}, u32[]{:S(2)}) copy-start(f32[8192,128]{1,0:T(8,128)} %a_ref.1) | copy-start | bytes 12582916
  2.8 0.9 copy-start.1

commit v3 on v2

--- a/solution.py
+++ b/solution.py
@@ -9,7 +9,7 @@
 
 HIGHEST = lax.Precision.HIGHEST
 PLANE = 4
-AHEAD = 4
+AHEAD = 16
 
 
 def exchange_kernel(
@@ -147,13 +147,19 @@
 
             rs_copy(way, w, j).start()
 
-        @pl.when(line - 1 - t > z)
+        to_right = line - 1 - t > z
+
+        @pl.when(jnp.logical_and(to_right, z < line // 2))
         def _():
             pass_on(0, line - 1 - t, has_left)
 
         @pl.when(jnp.logical_and(t < z, t < line - 1))
         def _():
             pass_on(1, t, has_right)
+
+        @pl.when(jnp.logical_and(to_right, z >= line // 2))
+        def _():
+            pass_on(0, line - 1 - t, has_left)
 
         @pl.when(t == line - 1)
         def _():

time: 131 us -> 114 us (0.87)
  Pallas kernels: 127 us -> 110 us
    pallas_call x1, Pallas kernels: 116 us -> 99.5 us  [exchange(): pl.pallas_call(functools.partial(exchange_kernel, line, parts, sub), out_...]
where the time goes in v3:
time: 114 us
  Pallas kernels  110 us (96%)
  local copies, waits for them, and re-layouts  3.08 us (3%)
    pallas_call x1, Pallas kernels, exchange(): pl.pallas_call(functools.partial(exchange_kernel, line, parts, sub), out_...  99.5 us
    pallas_call x1, Pallas kernels, local(): pl.pallas_call(functools.partial(factor_kernel, float(channels) ** 0.5),...  10.9 us
    unnamed x4, local copies, waits for them, and re-layouts  3.08 us

profile of v3, /device:TPU:0, one launch (start us, length us, event | category | flops | bytes accessed | tf_op | source)
XLA Modules:
  0.0 114.1 jit_solution(12916926483129075374)
XLA Ops:
  0.6 0.0 copy-start
  0.6 2.2 %copy-done = f32[8192,128]{1,0:T(8,128)S(1)} copy-done((f32[8192,128]{1,0:T(8,128)S(1)}, f32[8192,128]{1,0:T(8,128)}, u32[]{:S(2)}) %copy-start) | copy-done | bytes 4194328
  2.8 0.0 copy-start.1
  2.8 0.9 copy-done.1
  3.7 99.5 %shard_map.41 = (f32[512,256]{1,0:T(8,128)S(1)}, f32[256,256]{1,0:T(8,128)S(1)}, f32[256,128]{1,0:T(8,128)S(1)}) custom-call(f32[8192,128]{1,0:T(8,128)S(1)} %copy-done, f32[128,256]{1,0:T(8,128)S(1)} %copy-done.1), custom_call_target="tpu_custom_call" | custom-call | tf_op jit(solution)/shard_map/pallas_call | solution.py:279
  103.2 10.9 %shard_map.42 = (f32[512,256]{1,0:T(8,128)}, f32[256,128]{1,0:T(8,128)}) custom-call(f32[512,256]{1,0:T(8,128)S(1)} %get-tuple-element.5.y_ref, f32[256,256]{1,0:T(8,128)S(1)} %get-tuple-element.6.g_ref, f32[256,128]{1,0:T(8,128)S(1)} %get-tuple-element.7.p_ref), custom_call_target="tpu_custom_call" | custom-call | tf_op jit(solution)/shard_map/pallas_call | solution.py:379
Async XLA Ops:
  0.6 2.2 %copy-start = (f32[8192,128]{1,0:T(8,128)S(1)}, f32[8192,128]{1,0:T(8,128)}, u32[]{:S(2)}) copy-start(f32[8192,128]{1,0:T(8,128)} %a_ref.1) | copy-start | bytes 12582916
  2.8 0.9 copy-start.1

commit v4 on v3

--- a/solution.py
+++ b/solution.py
@@ -180,12 +180,16 @@
             def _():
                 ag_copy(1, z, j).start()
 
-            use(z, j)
-
         return 0
 
     lax.fori_loop(0, steps, reduce_step, 0)
     y_out[...] = full[z]
+
+    def own_step(j, _):
+        use(z, j)
+        return 0
+
+    lax.fori_loop(0, parts, own_step, 0)
 
     def gather_step(step, _):
         t, j = step // parts + 1, step % parts

time: 114 us -> 115 us (level)
  no operation moved by 1% of the time
where the time goes in v4:
time: 115 us
  Pallas kernels  111 us (97%)
  local copies, waits for them, and re-layouts  3.08 us (3%)
    pallas_call x1, Pallas kernels, exchange(): pl.pallas_call(functools.partial(exchange_kernel, line, parts, sub), out_...  101 us
    pallas_call x1, Pallas kernels, local(): pl.pallas_call(functools.partial(factor_kernel, float(channels) ** 0.5),...  10.9 us
    unnamed x4, local copies, waits for them, and re-layouts  3.08 us

profile of v4, /device:TPU:0, one launch (start us, length us, event | category | flops | bytes accessed | tf_op | source)
XLA Modules:
  0.0 115.2 jit_solution(17277290565993125510)
XLA Ops:
  0.6 0.0 copy-start
  0.6 2.2 %copy-done = f32[8192,128]{1,0:T(8,128)S(1)} copy-done((f32[8192,128]{1,0:T(8,128)S(1)}, f32[8192,128]{1,0:T(8,128)}, u32[]{:S(2)}) %copy-start) | copy-done | bytes 4194328
  2.8 0.0 copy-start.1
  2.8 0.9 copy-done.1
  3.7 100.5 %shard_map.41 = (f32[512,256]{1,0:T(8,128)S(1)}, f32[256,256]{1,0:T(8,128)S(1)}, f32[256,128]{1,0:T(8,128)S(1)}) custom-call(f32[8192,128]{1,0:T(8,128)S(1)} %copy-done, f32[128,256]{1,0:T(8,128)S(1)} %copy-done.1), custom_call_target="tpu_custom_call" | custom-call | tf_op jit(solution)/shard_map/pallas_call | solution.py:283
  104.3 10.9 %shard_map.42 = (f32[512,256]{1,0:T(8,128)}, f32[256,128]{1,0:T(8,128)}) custom-call(f32[512,256]{1,0:T(8,128)S(1)} %get-tuple-element.5.y_ref, f32[256,256]{1,0:T(8,128)S(1)} %get-tuple-element.6.g_ref, f32[256,128]{1,0:T(8,128)S(1)} %get-tuple-element.7.p_ref), custom_call_target="tpu_custom_call" | custom-call | tf_op jit(solution)/shard_map/pallas_call | solution.py:383
Async XLA Ops:
  0.6 2.2 %copy-start = (f32[8192,128]{1,0:T(8,128)S(1)}, f32[8192,128]{1,0:T(8,128)}, u32[]{:S(2)}) copy-start(f32[8192,128]{1,0:T(8,128)} %a_ref.1) | copy-start | bytes 12582916
  2.8 0.9 copy-start.1
